TPU v7x, 512 devices: a whole 4x8x8 slice. The times are simulated.
512 devices in a mesh: dpa: 16 (over x, y_hi, core), dpb: 32 (over z, y_lo).
Axes of the slice: x: 4, y: 8 (y_hi: 2, y_lo: 4; y = y_hi * 4 + y_lo), z: 8, core: 2. Of those that a mesh axis runs over, the one named last changes fastest.
Arguments:
- activations: bfloat16 [262144, 640], P(('dpa', 'dpb')), may hold values from -6 to 6
- upstream: bfloat16 [262144, 640], P(('dpa', 'dpb')), may hold values from -6 to 6
- norm_gain: float32 [1, 640], replicated, may hold values from -0.5 to 0.5
- weight_shards: bfloat16 [1, 1966080], P(None, 'dpa'), may hold values from -0.25 to 0.25
- master: float32 [1, 1966080], P(None, ('dpa', 'dpb')), may hold values from -0.25 to 0.25
- moment_one: float32 [1, 1966080], P(None, ('dpa', 'dpb')), may hold values from -6 to 6
- moment_two: float32 [1, 1966080], P(None, ('dpa', 'dpb')), may hold values from 1 to 16
Outputs:
- grad_input: bfloat16 [262144, 640], P(('dpa', 'dpb'))
- gradient: float32 [1, 1966080], P(None, ('dpa', 'dpb'))
- new_weights: bfloat16 [1, 1966080], P(None, 'dpa')
- new_master: float32 [1, 1966080], P(None, ('dpa', 'dpb'))
- new_moment_one: float32 [1, 1966080], P(None, ('dpa', 'dpb'))
- new_moment_two: float32 [1, 1966080], P(None, ('dpa', 'dpb'))
All inputs are finite; a program needn't handle non-finite values.
Results may differ from a plain program's by a relative error of at most 0.02.
Values may be sent and summed in bfloat16 or wider, within the bound.
A program may use at most 64 MiB of HBM per device.

v0:
```python
import jax
import jax.numpy as jnp
from jax import lax
from jax.sharding import PartitionSpec as P


def backward_layer(inputs, packed, gain, cotangent):
    hidden_count = packed.shape[0] // 3
    residual = inputs.astype(jnp.float32)
    inv_rms = lax.rsqrt(jnp.mean(residual * residual, axis=-1, keepdims=True) + 1e-06)
    normed = residual * inv_rms
    gain_row = 1.0 + gain
    hidden_in = (normed * gain_row).astype(jnp.bfloat16)
    projected = lax.dot_general(
        hidden_in,
        packed[: 2 * hidden_count],
        (((1,), (1,)), ((), ())),
        preferred_element_type=jnp.float32,
    )
    gate_pre = projected[:, :hidden_count]
    up_pre = projected[:, hidden_count:]
    activated, pullback = jax.vjp(lambda values: jax.nn.gelu(values, approximate=True), gate_pre)
    mixed = (activated * up_pre).astype(jnp.bfloat16)
    out_rows = packed[2 * hidden_count :]
    d_mixed = lax.dot_general(
        cotangent, out_rows, (((1,), (1,)), ((), ())), preferred_element_type=jnp.float32
    )
    grad_out = lax.dot_general(
        mixed, cotangent, (((0,), (0,)), ((), ())), preferred_element_type=jnp.float32
    )
    d_gate = pullback(d_mixed * up_pre)[0]
    d_up = d_mixed * activated
    d_projected = jnp.concatenate([d_gate, d_up], axis=1).astype(jnp.bfloat16)
    grad_in = lax.dot_general(
        d_projected, hidden_in, (((0,), (0,)), ((), ())), preferred_element_type=jnp.float32
    )
    d_hidden = jnp.dot(d_projected, packed[: 2 * hidden_count], preferred_element_type=jnp.float32)
    d_normed = d_hidden * gain_row
    passed = cotangent.astype(jnp.float32) + inv_rms * (
        d_normed - normed * jnp.mean(d_normed * normed, axis=-1, keepdims=True)
    )
    gradient = jnp.concatenate([grad_in, grad_out], axis=0).reshape(-1)
    return (passed.astype(jnp.bfloat16), gradient)


def reduce_grad(gradient):
    partial_value = lax.psum_scatter(
        gradient.astype(jnp.bfloat16), "dpa", scatter_dimension=0, tiled=True
    ).astype(jnp.float32)
    return lax.psum_scatter(partial_value, "dpb", scatter_dimension=0, tiled=True)


def shards(activations, upstream, norm_gain, weight_shards, master, moment_one, moment_two):
    count_first = lax.axis_size("dpa")
    count_second = lax.axis_size("dpb")
    layers = weight_shards.shape[0]
    width_model = activations.shape[1]
    gathered = lax.all_gather(weight_shards, "dpa", axis=1, tiled=True)
    packed_all = gathered.reshape(layers, gathered.shape[1] // width_model, width_model)
    inputs_list = [activations]
    cotangent = upstream
    owned_grads = [None] * layers
    for layer_no in reversed(range(layers)):
        cotangent, gradient = backward_layer(
            inputs_list[layer_no], packed_all[layer_no], norm_gain[layer_no], cotangent
        )
        rounded = gradient.astype(jnp.bfloat16).astype(jnp.float32)
        owned_grads[layer_no] = reduce_grad(rounded) / (count_first * count_second)
    gradients = jnp.stack(owned_grads)
    new_moment_one = 0.9 * moment_one + 0.1 * gradients
    new_moment_two = 0.95 * moment_two + 0.05 * gradients * gradients
    new_master = master - 0.01 * (
        new_moment_one / (jnp.sqrt(new_moment_two) + 1e-08) + 0.1 * master
    )
    new_weights = lax.all_gather(new_master.astype(jnp.bfloat16), "dpb", axis=1, tiled=True)
    return (cotangent, gradients, new_weights, new_master, new_moment_one, new_moment_two)


def solution(mesh):
    placed = (
        P(("dpa", "dpb"), None),
        P(("dpa", "dpb"), None),
        P(),
        P(None, "dpa"),
        P(None, ("dpa", "dpb")),
        P(None, ("dpa", "dpb")),
        P(None, ("dpa", "dpb")),
    )
    return jax.shard_map(
        shards,
        mesh=mesh,
        in_specs=placed,
        out_specs=(
            P(("dpa", "dpb"), None),
            P(None, ("dpa", "dpb")),
            P(None, "dpa"),
            P(None, ("dpa", "dpb")),
            P(None, ("dpa", "dpb")),
            P(None, ("dpa", "dpb")),
        ),
        check_vma=False,
    )
```

profile of v0, /device:TPU:4, one launch (start us, length us, event | category | flops | bytes accessed | tf_op | source)
XLA Modules:
  0.0 847.6 jit_solution(11857443303624054659)
XLA Ops:
  7.2 0.0 all-gather.2.cloned.1.call-start
  7.2 0.7 all-gather.2.cloned.1.call-update
  7.9 0.0 all-reduce.5.cloned.1.call-start
  7.9 0.7 add_reduce_fusion
  8.6 1.3 fusion.16
  9.9 112.5 %all-gather.2.cloned.1.call-done = bf16[1,1966080]{1,0:T(2,128)(2,1)} async-done(((bf16[1,122880]{1,0:T(2,128)(2,1)}), bf16[1,1966080]{1,0:T(2,128)(2,1)}) %all-gather.2.cloned.1.call-update) | async-done | bytes 3932176 | tf_op jit(solution)/shard_map/all_gather | solution.py:58
  122.5 44.8 %slice_reduce_fusion = bf16[1310720]{0:T(1024)(128)(2,1)S(1)} fusion(bf16[1,1966080]{1,0:T(2,128)(2,1)} %all-gather.2.cloned.1.call-done), kind=kLoop, calls=%fused_computation | loop fusion | bytes 5242880 | tf_op jit(solution)/shard_map/slice | solution.py:16
  167.2 3.2 slice.22
  170.4 22.9 %slice_reduce_fusion.1 = bf16[655360]{0:T(1024)(128)(2,1)S(1)} fusion(bf16[1,1966080]{1,0:T(2,128)(2,1)} %all-gather.2.cloned.1.call-done), kind=kLoop, calls=%fused_computation.5 | loop fusion | bytes 2621440 | tf_op jit(solution)/shard_map/slice | solution.py:24
  193.3 0.0 copy-start.1
  193.3 1.2 slice.20
  194.5 0.0 copy-done.1
  194.5 0.0 copy-start.2
  194.5 3.7 fusion.18
  198.2 0.0 copy-done.2
  198.2 1.4 convolution_convert_fusion.1
  199.6 2.5 fusion.6
  202.1 0.0 copy-start.6
  202.1 0.0 copy-start.7
  202.1 1.0 copy-done.6
  203.1 0.3 copy-done.7
  203.4 2.0 convolution_convert_fusion
  205.4 2.2 pad_maximum_fusion
  207.6 7.4 convert_element_type.33
  215.0 0.0 copy-start
  215.0 0.0 all-reduce.5.cloned.1.call-update
  215.0 0.0 all-reduce.7.cloned.1.call-start
  215.1 1.4 dynamic-slice.2
  216.5 1.3 dynamic-slice
  219.1 0.0 copy-done
  219.1 4.5 fusion.11
  223.6 221.1 %all-reduce.5.cloned.1.call-done = bf16[1966080]{0:T(1024)(128)(2,1)} async-done(((bf16[1966080]{0:T(1024)(128)(2,1)}), bf16[1966080]{0:T(1024)(128)(2,1)}) %all-reduce.5.cloned.1.call-update) | async-done | bytes 3932176
  444.7 1.8 dynamic-slice_convert_fusion
  446.4 0.0 copy-start.3
  446.4 0.0 copy-start.4
  446.4 0.0 copy-start.5
  446.4 0.0 all-reduce.7.cloned.1.call-update
  446.5 2.7 fusion.15
  449.2 309.1 %all-reduce.7.cloned.1.call-done = f32[122880]{0:T(1024)} async-done(((f32[122880]{0:T(1024)}), f32[122880]{0:T(1024)}) %all-reduce.7.cloned.1.call-update) | async-done | bytes 491536
  758.3 0.8 dynamic-slice_multiply_fusion
  759.1 0.6 stack.3
  759.7 0.0 copy-done.3
  759.7 0.0 copy-done.4
  759.7 0.0 copy-done.5
  759.7 0.7 fusion.26
  760.4 80.0 %all_gather.7 = bf16[1,122880]{1,0:T(2,128)(2,1)S(1)} all-gather(bf16[1,3840]{1,0:T(2,128)(2,1)S(1)} %get-tuple-element.6), channel_id=1, replica_groups=mesh['dpa'=16,'dpb'=32] {'dpb'}, dimensions={1}, use_global_device_ids=true | all-gather | bytes 253440 | tf_op jit(solution)/shard_map/all_gather | solution.py:75
  840.3 0.8 copy.16
  (2 shorter events, 0.0 us)
Async XLA Ops:
  7.2 115.3 %all-gather.2.cloned.1.call-start = ((), (), s32[]{:S(2)}) async-start(), calls=%async_computation | async-start | bytes 8355840 | tf_op jit(solution)/shard_map/all_gather | solution.py:58
  7.9 436.8 %all-reduce.5.cloned.1.call-start = ((), (), s32[]{:S(2)}) async-start(), calls=%async_computation.1 | async-start | bytes 7864320
  193.3 1.2 copy-start.1
  194.5 3.7 copy-start.2
  202.1 1.0 copy-start.6
  202.1 1.3 copy-start.7
  215.0 4.1 copy-start
  215.0 543.2 %all-reduce.7.cloned.1.call-start = ((), (), s32[]{:S(2)}) async-start(), calls=%async_computation.2 | async-start | bytes 983040
  446.4 313.2 %copy-start.3 = (f32[1,3840]{1,0:T(1,128)S(1)}, f32[1,3840]{1,0:T(1,128)}, u32[]{:S(2)}) copy-start(f32[1,3840]{1,0:T(1,128)} %param.11) | copy-start | bytes 46084
  446.4 313.3 %copy-start.4 = (f32[1,3840]{1,0:T(1,128)S(1)}, f32[1,3840]{1,0:T(1,128)}, u32[]{:S(2)}) copy-start(f32[1,3840]{1,0:T(1,128)} %param.13) | copy-start | bytes 46084
  446.4 313.3 %copy-start.5 = (f32[1,3840]{1,0:T(1,128)S(1)}, f32[1,3840]{1,0:T(1,128)}, u32[]{:S(2)}) copy-start(f32[1,3840]{1,0:T(1,128)} %param.12) | copy-start | bytes 46084
Sparse Core Ops, SparseCore 0:
  11.3 111.1 all-gather.1
  215.1 229.4 all-reduce.4
  448.4 309.7 all-reduce.6
where the time goes:
time: 848 us
  waiting for transfers between devices  643 us (76%)
  local copies, waits for them, and re-layouts  84.8 us (10%)
  blocking collectives  80 us (9%)
  between operations  15.2 us (2%)
  matrix products  14 us (2%)
  other arithmetic  10.2 us (1%)
    unnamed x5, waiting for transfers between devices  531 us
    all_gather x1, waiting for transfers between devices, shards(): gathered = lax.all_gather(weight_shards, 'dpa', axis=1, tiled=True)  113 us
    all_gather x1, blocking collectives, shards(): lax.all_gather(new_master.astype(jnp.bfloat16), 'dpb', axis=1, tiled=True)  80 us
    slice x2, local copies, waits for them, and re-layouts, backward_layer(): packed[:2 * hidden_count]  47.9 us
    slice x2, local copies, waits for them, and re-layouts, backward_layer(): out_rows = packed[2 * hidden_count:]  24.1 us
  transfers between devices with their start and end apart: 3, of which 3 were waited for; matrix products, arithmetic and copies ran while one was open for 1% of the time, Pallas kernels for 0%

commit v1 on v0

v1 whole, which is shorter than its diff:
```python
import math

import jax
import jax.numpy as jnp
from jax import lax
from jax.experimental import pallas as pl
from jax.experimental.pallas import tpu as pltpu
from jax.sharding import PartitionSpec as P

BF16 = jnp.bfloat16
F32 = jnp.float32
MESH = pl.DeviceIdType.MESH

D = 640
TOK = 512
NX, NY, NZ, NQ = 4, 8, 8, 4
BLK = 64
COLS = ((0, 256), (256, 256), (512, 128))

NT = (((1,), (1,)), ((), ()))
TN = (((0,), (0,)), ((), ()))

GELU_K = math.sqrt(2.0 / math.pi)


def mesh_kernel(
    act, up, gain, wsh, mas, mo1, mo2,
    gin_o, grad_o, nw_o, nm_o, n1_o, n2_o,
    xin, cin, hc, wt, pt, g4, s2, xr, yr, tsum, zs, zb, zr, nb, dh, dhr, invr,
    act_s, act_r, a1_s, a1_r, ya_s, ya_r, xa_s, xa_r, rl_s, rl_r, xg_s, xg_r, yg_s, yg_r,
    zg_s, zg_r, dh_s, dh_r, nw_s, nw_r,
):
    a = lax.axis_index("dpa")
    b = lax.axis_index("dpb")
    x, yh, c = a // 4, (a // 2) % 2, a % 2
    z, q = b // 4, b % 4
    y = yh * 4 + q

    def dev(dx=0, dy=0, z_to=None, y_to=None, c_to=None):
        xt = (x + dx + NX) % NX
        yt = (y + dy + NY) % NY if y_to is None else y_to
        zt = z if z_to is None else z_to
        ct = c if c_to is None else c_to
        return {"dpa": (xt * 2 + yt // 4) * 2 + ct, "dpb": zt * 4 + yt % 4}

    def copy(src, dst, s, r, to):
        return pltpu.make_async_remote_copy(
            src_ref=src, dst_ref=dst, send_sem=s, recv_sem=r, device_id=to, device_id_type=MESH
        )

    barrier = pltpu.get_barrier_semaphore()
    peers = [dev(c_to=1 - c), dev(dx=1), dev(dx=-1)]
    peers += [dev(dy=d) for d in range(1, NY)]
    peers += [dev(z_to=(z + d) % NZ) for d in range(1, NZ)]
    for to in peers:
        pl.semaphore_signal(barrier, inc=1, device_id=to, device_id_type=MESH)

    mine = pl.multiple_of(c * TOK, TOK)
    own_t = 3 * (2 * x + yh)
    xin[pl.ds(mine, TOK), :] = act[...]
    cin[pl.ds(mine, TOK), :] = up[...]
    wt[own_t + c] = wsh[0]
    wt[own_t + c + 1] = wsh[2]
    pl.semaphore_wait(barrier, len(peers))

    other = dev(c_to=1 - c)
    a1 = copy(wsh.at[1], wt.at[own_t + 2 * c], a1_s, a1_r, other)
    a1.start()
    acts = [
        copy(ref.at[pl.ds(mine, TOK)], ref.at[pl.ds(mine, TOK)], act_s.at[i], act_r.at[i], other)
        for i, ref in enumerate((xin, cin))
    ]
    for cp in acts:
        cp.start()
    a1.wait()

    def shard(xx, hh):
        return wt.at[pl.ds(3 * (2 * ((xx + NX) % NX) + hh), 3)]

    def shard_part(xx, hh, start, n):
        return wt.at[pl.ds(3 * (2 * ((xx + NX) % NX) + hh) + start, n)]

    left, right = dev(dx=-1), dev(dx=1)
    x_copies = []

    def x_share(hh, k):
        for j, to in enumerate((right, left)):
            cp = copy(shard(x, hh), shard(x, hh), xa_s.at[k, j], xa_r.at[k, j], to)
            cp.start()
            x_copies.append(cp)

    def x_forward(hh, k):
        cut = 2 if k == 0 else 1
        copy(shard(x - 1, hh), shard(x - 1, hh), xa_s.at[k, 0], xa_r.at[k, 0], right).wait_recv()
        part = shard_part(x - 1, hh, 0, cut)
        cp = copy(part, part, xa_s.at[k, 2], xa_r.at[k, 2], right)
        cp.start()
        x_copies.append(cp)
        copy(shard(x + 1, hh), shard(x + 1, hh), xa_s.at[k, 1], xa_r.at[k, 1], left).wait_recv()
        part = shard_part(x + 1, hh, cut, 3 - cut)
        cp = copy(part, part, xa_s.at[k, 3], xa_r.at[k, 3], left)
        cp.start()
        x_copies.append(cp)

    def x_finish(hh, k):
        cut = 2 if k == 0 else 1
        part = shard_part(x + 2, hh, 0, cut)
        copy(part, part, xa_s.at[k, 2], xa_r.at[k, 2], right).wait_recv()
        part = shard_part(x + 2, hh, cut, 3 - cut)
        copy(part, part, xa_s.at[k, 3], xa_r.at[k, 3], left).wait_recv()

    x_share(yh, 0)
    sign = jnp.where(q == 0, -1, 1)
    edge = (q == 0) | (q == NQ - 1)
    y_copies = [
        copy(shard(x, yh), shard(x, yh), ya_s.at[i], ya_r, dev(dy=sign * (i + 1))) for i in range(2)
    ]

    @pl.when(edge)
    def _():
        for cp in y_copies:
            cp.start()

    def norm(t0):
        def step(i, _):
            rows = pl.ds(pl.multiple_of(t0 + i * 128, 128), 128)
            v = xin[rows, :].astype(F32)
            s = lax.rsqrt(jnp.mean(v * v, axis=-1, keepdims=True) + 1e-6)
            invr[rows, :] = jnp.broadcast_to(s, (128, 128))
            hc[0, rows, :] = (v * s * (1.0 + gain[...])).astype(BF16)
            hc[1, rows, :] = cin[rows, :]
            return 0

        lax.fori_loop(0, TOK // 128, step, 0)

    norm(mine)
    x_forward(yh, 0)
    copy(shard(x, 1 - yh), shard(x, 1 - yh), ya_s.at[0], ya_r, right).wait_recv()
    x_share(1 - yh, 1)
    theirs = pl.multiple_of((1 - c) * TOK, TOK)
    for cp, ref in zip(acts, (xin, cin)):
        cp.wait()
    norm(theirs)
    x_forward(1 - yh, 1)
    x_finish(yh, 0)
    x_finish(1 - yh, 1)
    for cp in x_copies:
        cp.wait_send()

    @pl.when(edge)
    def _():
        for cp in y_copies:
            cp.wait_send()

    def hidden(i, _):
        u, t = i // 4, i % 4
        toks = pl.ds(pl.multiple_of(t * 256, 256), 256)
        hb, cb = hc[0, toks, :], hc[1, toks, :]

        def rows(kind):
            return wt[pl.ds(8 * kind + 4 * u, 4)].reshape(256, D)

        pa = lax.dot_general(rows(0), hb, NT, preferred_element_type=F32)
        pb = lax.dot_general(rows(1), hb, NT, preferred_element_type=F32)
        dz = lax.dot_general(rows(2), cb, NT, preferred_element_type=F32)
        sq = pa * pa
        th = jnp.tanh(GELU_K * (pa + 0.044715 * (sq * pa)))
        half = 0.5 * (1.0 + th)
        gelu = pa * half
        slope = half + (0.5 * GELU_K) * pa * (1.0 - th * th) * (1.0 + (3 * 0.044715) * sq)
        for kind, val in enumerate((slope * (dz * pb), dz * gelu, gelu * pb)):
            at = pl.ds(pl.multiple_of(512 * kind + 256 * u, 256), 256)
            pt[at, toks] = val.astype(BF16)
        return 0

    lax.fori_loop(0, 8, hidden, 0)

    relocs = []

    def grad_rows(k, dx):
        xt = (x + dx) % NX
        for i in range(3):
            n = 3 * xt + i
            val = jnp.dot(
                pt[pl.ds(pl.multiple_of(128 * n, 128), 128), :],
                hc[jnp.where(n < 8, 0, 1)],
                preferred_element_type=F32,
            ).astype(BF16)
            for e in range(2):
                m, j = divmod(2 * i + e, 3)
                slot = jnp.where(c == 0, (0, 2, 3)[j], (3, 0, 2)[j])
                g4[2 * xt + m, slot] = val[64 * e : 64 * (e + 1)]
        cp = copy(
            g4.at[pl.ds(2 * xt, 2), 3], g4.at[pl.ds(2 * xt, 2), 1], rl_s.at[k], rl_r.at[k], other
        )
        cp.start()
        relocs.append(cp)

    def part(m, p):
        return g4.at[m, pl.ds(0, 3), :, pl.ds(COLS[p][0], COLS[p][1])]

    def xbuf(i, p):
        return xr.at[i, :, :, pl.ds(COLS[p][0], COLS[p][1])]

    x_grad = []

    def x_send(src, i, p, to):
        cp = copy(src, xbuf(i, p), xg_s.at[i, p], xg_r.at[i, p], to)
        cp.start()
        x_grad.append(cp)

    def x_wait(i, p):
        copy(xbuf(i, p), xbuf(i, p), xg_s.at[i, p], xg_r.at[i, p], right).wait_recv()

    pieces = range(len(COLS))
    far, near_r, near_l = (x + 2) % NX, (x + 1) % NX, (x + 3) % NX
    grad_rows(0, 2)
    relocs[0].wait_recv()
    for p in pieces:
        x_send(part(2 * far, p), 0, p, right)
        x_send(part(2 * far + 1, p), 1, p, left)
    grad_rows(1, 1)
    grad_rows(2, 3)
    relocs[1].wait_recv()
    relocs[2].wait_recv()
    for p in pieces:
        x_send(part(2 * near_r + 1, p), 2, p, right)
        x_send(part(2 * near_l, p), 3, p, left)
    grad_rows(3, 0)

    for p in pieces:
        cols = pl.ds(COLS[p][0], COLS[p][1])
        for i, m, to in ((0, 2 * near_r, right), (1, 2 * near_l + 1, left)):
            x_wait(i, p)
            tot = g4[m, 0:3, :, cols].astype(F32) + xr[i, :, :, cols].astype(F32)
            g4[m, 0:3, :, cols] = tot.astype(BF16)
            x_send(part(m, p), 4 + i, p, to)

    def dh_rows(t0):
        def step(i, _):
            toks = pl.ds(pl.multiple_of(t0 + i * 256, 256), 256)
            dh[toks, :] = lax.dot_general(
                pt[pl.ds(0, 1024), toks], wt[0:16].reshape(1024, D), TN, preferred_element_type=F32
            )
            return 0

        lax.fori_loop(0, 2, step, 0)

    dh_rows(theirs)
    dh_copy = copy(dh.at[pl.ds(theirs, TOK)], dhr, dh_s, dh_r, other)
    dh_copy.start()
    dh_rows(mine)
    relocs[3].wait_recv()

    y_grad = []
    for p in pieces:
        cols = pl.ds(COLS[p][0], COLS[p][1])
        for i, (one, two) in enumerate(((4, 3), (2, 5))):
            x_wait(one, p)
            x_wait(two, p)
            tot = g4[2 * x + i, 0:3, :, cols].astype(F32) + xr[one, :, :, cols].astype(F32)
            tot = tot + xr[two, :, :, cols].astype(F32)
            s2[i, :, cols] = tot.reshape(192, COLS[p][1]).astype(BF16)
        for d in range(1, NY):
            yt = (y + d) % NY
            cp = copy(
                s2.at[yt // 4, pl.ds(pl.multiple_of(48 * (yt % 4), 16), 48), cols],
                yr.at[d, :, cols],
                yg_s.at[d, p],
                yg_r.at[d, p],
                dev(dy=d),
            )
            cp.start()
            y_grad.append(cp)

    dh_copy.wait()

    def finish_input(i, _):
        loc = pl.ds(pl.multiple_of(i * 128, 128), 128)
        rows = pl.ds(pl.multiple_of(mine + i * 128, 128), 128)
        dn = (dh[rows, :] + dhr[loc, :]) * (1.0 + gain[...])
        s = invr[rows, 0:1]
        n = xin[rows, :].astype(F32) * s
        mean = jnp.mean(dn * n, axis=-1, keepdims=True)
        gin_o[loc, :] = (cin[rows, :].astype(F32) + s * (dn - n * mean)).astype(BF16)
        return 0

    lax.fori_loop(0, TOK // 128, finish_input, 0)

    own = pl.ds(pl.multiple_of(48 * q, 16), 48)
    for p in pieces:
        cols = pl.ds(COLS[p][0], COLS[p][1])
        tot = s2[yh, own, cols].astype(F32)
        for d in range(1, NY):
            copy(
                yr.at[d, :, cols], yr.at[d, :, cols], yg_s.at[d, p], yg_r.at[d, p], right
            ).wait_recv()
            tot = tot + yr[d, :, cols].astype(F32)
        tsum[:, cols] = tot

    zs[...] = jnp.zeros_like(zs)
    for r in range(48):
        blk, jj = divmod(r, 6)
        for w in range(5):
            zs[blk, pl.ds(5 * jj + w, 1), :] = tsum[pl.ds(r, 1), pl.ds(128 * w, 128)]
    zb[...] = zs[...].astype(BF16)
    for e in range(2):
        for qt in range(NQ):
            zt = 2 * q + e
            self = (zt == z) & (q == qt)

            @pl.when(jnp.logical_not(self))
            def _():
                copy(
                    zb.at[e * 4 + qt], zr.at[z], zg_s.at[e * 4 + qt], zg_r.at[z],
                    dev(z_to=zt, y_to=yh * 4 + qt),
                ).start()

            @pl.when(self)
            def _():
                zr[z] = zb[e * 4 + qt]

    tot = jnp.zeros((32, 128), F32)
    for zf in range(NZ):
        self = (z // 2 == q) & (z == zf)

        @pl.when(jnp.logical_not(self))
        def _():
            copy(zr.at[zf], zr.at[zf], zg_s.at[0], zg_r.at[zf], right).wait_recv()

        tot = tot + zr[zf].astype(F32)

    grad = tot[0:30] * (1.0 / 512.0)
    n1 = 0.9 * mo1[...] + 0.1 * grad
    n2 = 0.95 * mo2[...] + 0.05 * grad * grad
    nm = mas[...] - 0.01 * (n1 / (jnp.sqrt(n2) + 1e-8) + 0.1 * mas[...])
    nb[pl.ds(0, 30), :] = nm
    nb[pl.ds(30, 2), :] = jnp.zeros((2, 128), F32)
    nw_o[b] = nb[...].astype(BF16)
    new = []
    for dz in range(NZ):
        for dq in range(NQ):
            if dz or dq:
                zt = (z + dz) % NZ
                cp = copy(
                    nw_o.at[b], nw_o.at[b], nw_s.at[dz, dq], nw_r.at[dz, dq],
                    dev(z_to=zt, y_to=yh * 4 + (q + dq) % NQ),
                )
                cp.start()
                new.append(cp)
    grad_o[...] = grad
    n1_o[...] = n1
    n2_o[...] = n2
    nm_o[...] = nm

    for cp in relocs + x_grad + y_grad:
        cp.wait_send()
    for e in range(2):
        for qt in range(NQ):
            self = (2 * q + e == z) & (q == qt)

            @pl.when(jnp.logical_not(self))
            def _():
                copy(zb.at[e * 4 + qt], zr.at[z], zg_s.at[e * 4 + qt], zg_r.at[z], right).wait_send()

    for dz in range(NZ):
        for dq in range(NQ):
            if dz or dq:
                bf = ((z - dz + NZ) % NZ) * 4 + (q - dq + NQ) % NQ
                copy(nw_o.at[bf], nw_o.at[bf], nw_s.at[dz, dq], nw_r.at[dz, dq], right).wait_recv()
    for cp in new:
        cp.wait_send()


def shards(activations, upstream, norm_gain, weight_shards, master, moment_one, moment_two):
    vm = pl.BlockSpec(memory_space=pltpu.VMEM)
    dma = pltpu.SemaphoreType.DMA
    np_ = len(COLS)
    state = [v.reshape(30, 128) for v in (master, moment_one, moment_two)]
    shape = jax.ShapeDtypeStruct
    gin, grad, nw, nm, n1, n2 = pl.pallas_call(
        mesh_kernel,
        out_shape=[
            shape((TOK, D), BF16),
            shape((30, 128), F32),
            shape((32, 32, 128), BF16),
            shape((30, 128), F32),
            shape((30, 128), F32),
            shape((30, 128), F32),
        ],
        in_specs=[vm] * 7,
        out_specs=[vm] * 6,
        scratch_shapes=[
            pltpu.VMEM((2 * TOK, D), BF16),
            pltpu.VMEM((2 * TOK, D), BF16),
            pltpu.VMEM((2, 2 * TOK, D), BF16),
            pltpu.VMEM((24, BLK, D), BF16),
            pltpu.VMEM((1536, 2 * TOK), BF16),
            pltpu.VMEM((8, 4, BLK, D), BF16),
            pltpu.VMEM((2, 192, D), BF16),
            pltpu.VMEM((6, 3, BLK, D), BF16),
            pltpu.VMEM((NY, 48, D), BF16),
            pltpu.VMEM((48, D), F32),
            pltpu.VMEM((8, 32, 128), F32),
            pltpu.VMEM((8, 32, 128), BF16),
            pltpu.VMEM((NZ, 32, 128), BF16),
            pltpu.VMEM((32, 128), F32),
            pltpu.VMEM((2 * TOK, D), F32),
            pltpu.VMEM((TOK, D), F32),
            pltpu.VMEM((2 * TOK, 128), F32),
            dma((2,)), dma((2,)),
            dma, dma,
            dma((2,)), dma,
            dma((2, 4)), dma((2, 4)),
            dma((4,)), dma((4,)),
            dma((6, np_)), dma((6, np_)),
            dma((NY, np_)), dma((NY, np_)),
            dma((8,)), dma((NZ,)),
            dma, dma,
            dma((NZ, NQ)), dma((NZ, NQ)),
        ],
        compiler_params=pltpu.CompilerParams(
            collective_id=0, has_side_effects=True, vmem_limit_bytes=56 * 1024 * 1024
        ),
        name="ffn_backward_adam",
    )(activations, upstream, norm_gain, weight_shards.reshape(3, BLK, D), *state)
    flat = lambda v: v.reshape(1, 3840)
    return (
        gin,
        flat(grad),
        nw[:, :30].reshape(1, 32 * 3840),
        flat(nm),
        flat(n1),
        flat(n2),
    )


def solution(mesh):
    own = P(None, ("dpa", "dpb"))
    rows = P(("dpa", "dpb"), None)
    return jax.shard_map(
        shards,
        mesh=mesh,
        in_specs=(rows, rows, P(), P(None, "dpa"), own, own, own),
        out_specs=(rows, own, P(None, "dpa"), own, own, own),
        check_vma=False,
    )
```

time: 848 us -> 106 us (0.12)
  the two profiles are of different devices: /device:TPU:4 before, /device:TPU:1 now
where the time goes in v1:
time: 106 us; the launch traced here: 105 us
  Pallas kernels  93.4 us (88%)
  local copies, waits for them, and re-layouts  6.53 us (6%)
  other arithmetic  4.3 us (4%)
    pallas_call x1, Pallas kernels, shards(): pl.pallas_call(mesh_kernel, out_shape=[shape((TOK, D), BF16), shape((30,...  93.4 us
    unnamed x4, other arithmetic  4.3 us
    reshape x2, local copies, waits for them, and re-layouts, shards(): flat = lambda v: v.reshape(1, 3840)  2.81 us

profile of v1, /device:TPU:1, one launch (start us, length us, event | category | flops | bytes accessed | tf_op | source)
XLA Modules:
  0.0 104.9 jit_solution(7097284998671322202)
XLA Ops:
  0.6 2.4 %reduce = bf16[122880]{0:T(1024)(128)(2,1)S(1)} reduce(bf16[1,122880]{1,0:T(2,128)(2,1)} %param.10, bf16[]{:T(256)} %constant.3), dimensions={0}, to_apply=%param.10.reduce_sub_computation | reduce | bytes 491522 | tf_op args[3]
  3.0 0.0 copy-start.1
  3.0 0.9 reshape.39.wsh
  3.9 0.0 copy-done.1
  3.9 0.0 copy-start.2
  3.9 0.6 reduce.1
  4.6 0.1 copy-done.2
  4.6 0.0 copy-start.3
  4.6 0.6 reduce.2
  5.3 0.1 copy-done.3
  5.3 0.6 reduce.3
  6.0 93.4 %ffn_backward_adam.1 = (bf16[512,640]{1,0:T(8,128)(2,1)}, f32[30,128]{1,0:T(8,128)}, bf16[32,32,128]{2,1,0:T(8,128)(2,1)}, f32[30,128]{1,0:T(8,128)}, f32[30,128]{1,0:T(8,128)}, /*index=5*/f32[30,128]{1,0:T(8,128)}) custom-call(bf16[512,640]{1,0:T(8,128)(2,1)} %act.1, bf16[512,640]{1,0:T(8,128)(2,1)} %up.1, f32[1,640]{1,0:T(1,128)} %gain.1, ...), custom_call_target="tpu_custom_call" | custom-call | tf_op jit(solution)/shard_map/ffn_backward_adam/pallas_call | solution.py:381
  99.4 0.0 copy-start
  99.4 1.4 %copy_bitcast_fusion = (f32[1,3840]{1,0:T(1,128)}, f32[1,3840]{1,0:T(1,128)}) fusion(f32[1,1,30,128]{3,2,1,0:T(8,128)} %bitcast.27, f32[1,1,30,128]{3,2,1,0:T(8,128)} %bitcast.26), kind=kLoop, calls=%fused_computation | loop fusion | bytes 61440 | tf_op jit(solution)/shard_map/reshape | solution.py:427
  100.8 1.4 %copy_bitcast_fusion.2 = (f32[1,3840]{1,0:T(1,128)}, f32[1,3840]{1,0:T(1,128)}) fusion(f32[1,1,30,128]{3,2,1,0:T(8,128)} %bitcast.25, f32[1,1,30,128]{3,2,1,0:T(8,128)} %bitcast.24), kind=kLoop, calls=%fused_computation.2 | loop fusion | bytes 61440 | tf_op jit(solution)/shard_map/reshape | solution.py:427
  102.2 1.8 %reshape.44 = bf16[1,122880]{1,0:T(2,128)(2,1)} reshape(bf16[32,30,128]{2,1,0:T(8,128)(2,1)} %bitcast.20) | data formatting | bytes 491520 | tf_op jit(solution)/shard_map/reshape | solution.py:431
  104.0 0.0 copy-done
  104.1 0.8 copy.22
Async XLA Ops:
  3.0 0.9 copy-start.1
  3.9 0.7 copy-start.2
  4.6 0.7 copy-start.3
  99.4 4.7 %copy-start = (bf16[512,640]{1,0:T(8,128)(2,1)S(1)}, bf16[512,640]{1,0:T(8,128)(2,1)}, u32[]{:S(2)}) copy-start(bf16[512,640]{1,0:T(8,128)(2,1)} %get-tuple-element.28) | copy-start | bytes 1966084

commit v2 on v1

--- a/solution.py
+++ b/solution.py
@@ -24,10 +24,10 @@
 
 
 def mesh_kernel(
-    act, up, gain, wsh, mas, mo1, mo2,
+    act, up, gain, wflat, mas, mo1, mo2,
     gin_o, grad_o, nw_o, nm_o, n1_o, n2_o,
-    xin, cin, hc, wt, pt, g4, s2, xr, yr, tsum, zs, zb, zr, nb, dh, dhr, invr,
-    act_s, act_r, a1_s, a1_r, ya_s, ya_r, xa_s, xa_r, rl_s, rl_r, xg_s, xg_r, yg_s, yg_r,
+    wf, wsh, state, nwr, xin, cin, hc, w2, pt, g4, s2, xr, yr, tsum, zs, zb, zr, nb, dh, dhr, invr,
+    act_s, act_r, a1_s, a1_r, ya_s, ya_r, xa_s, xa_r, xo_s, xo_r, za_s, za_r, rl_s, rl_r, xg_s, xg_r, yg_s, yg_r,
     zg_s, zg_r, dh_s, dh_r, nw_s, nw_r,
 ):
     a = lax.axis_index("dpa")
@@ -56,15 +56,26 @@
         pl.semaphore_signal(barrier, inc=1, device_id=to, device_id_type=MESH)
 
     mine = pl.multiple_of(c * TOK, TOK)
+    theirs = pl.multiple_of((1 - c) * TOK, TOK)
     own_t = 3 * (2 * x + yh)
+
+    def blocks(t, n=1):
+        return pl.ds(pl.multiple_of(BLK * t, BLK), BLK * n)
+
     xin[pl.ds(mine, TOK), :] = act[...]
     cin[pl.ds(mine, TOK), :] = up[...]
-    wt[own_t + c] = wsh[0]
-    wt[own_t + c + 1] = wsh[2]
+    for r in range(3 * BLK):
+        wf[pl.ds(r, 1), :] = wflat[:, pl.ds(D * r, D)].astype(F32)
+    w2[blocks(own_t + c)] = wf[0:64].astype(BF16)
+    wsh[...] = wf[64:128].astype(BF16)
+    w2[blocks(own_t + c + 1)] = wf[128:192].astype(BF16)
+    for i, ref in enumerate((mas, mo1, mo2)):
+        for r in range(30):
+            state[i, pl.ds(r, 1), :] = ref[:, pl.ds(128 * r, 128)]
     pl.semaphore_wait(barrier, len(peers))
 
     other = dev(c_to=1 - c)
-    a1 = copy(wsh.at[1], wt.at[own_t + 2 * c], a1_s, a1_r, other)
+    a1 = copy(wsh, w2.at[blocks(own_t + 2 * c)], a1_s, a1_r, other)
     a1.start()
     acts = [
         copy(ref.at[pl.ds(mine, TOK)], ref.at[pl.ds(mine, TOK)], act_s.at[i], act_r.at[i], other)
@@ -75,10 +86,11 @@
     a1.wait()
 
     def shard(xx, hh):
-        return wt.at[pl.ds(3 * (2 * ((xx + NX) % NX) + hh), 3)]
+        return shard_part(xx, hh, 0, 3)
 
     def shard_part(xx, hh, start, n):
-        return wt.at[pl.ds(3 * (2 * ((xx + NX) % NX) + hh) + start, n)]
+        at = 192 * (2 * ((xx + NX) % NX) + hh) + BLK * start
+        return w2.at[pl.ds(pl.multiple_of(at, BLK), BLK * n)]
 
     left, right = dev(dx=-1), dev(dx=1)
     x_copies = []
@@ -112,14 +124,34 @@
     x_share(yh, 0)
     sign = jnp.where(q == 0, -1, 1)
     edge = (q == 0) | (q == NQ - 1)
-    y_copies = [
-        copy(shard(x, yh), shard(x, yh), ya_s.at[i], ya_r, dev(dy=sign * (i + 1))) for i in range(2)
-    ]
+    odd = z % 2
+    oh = 1 - yh
+
+    def piece(xx, hh, h, k):
+        start = 192 * (2 * ((xx + NX) % NX) + hh) + 96 * h + 48 * k
+        return w2.at[pl.ds(pl.multiple_of(start, 16), 48)]
+
+    def send_piece(ref, s, r, to):
+        cp = copy(ref, ref, s, r, to)
+        cp.start()
+        x_copies.append(cp)
+
+    y_copies = []
+    for k in range(2):
+        for j in (1, 0):
+            ref = piece(x, yh, odd, k)
+            y_copies.append(copy(ref, ref, ya_s.at[k, j], ya_r.at[k], dev(dy=sign * (j + 1))))
 
     @pl.when(edge)
     def _():
         for cp in y_copies:
             cp.start()
+
+    up_z, down_z = dev(z_to=(z + 1) % NZ), dev(z_to=(z + NZ - 1) % NZ)
+
+    def z_send(dx, k):
+        ref = piece(x + dx, oh, odd, k)
+        send_piece(ref, za_s.at[dx, k], za_r.at[dx, k], (up_z, down_z)[k])
 
     def norm(t0):
         def step(i, _):
@@ -134,16 +166,32 @@
         lax.fori_loop(0, TOK // 128, step, 0)
 
     norm(mine)
+    for k in range(2):
+        ref = piece(x, oh, odd, k)
+        copy(ref, ref, ya_s.at[k, 0], ya_r.at[k], right).wait_recv()
+        for j, to in enumerate((right, left)):
+            send_piece(ref, xo_s.at[k, j], xo_r.at[k, j], to)
+        z_send(0, k)
     x_forward(yh, 0)
-    copy(shard(x, 1 - yh), shard(x, 1 - yh), ya_s.at[0], ya_r, right).wait_recv()
-    x_share(1 - yh, 1)
-    theirs = pl.multiple_of((1 - c) * TOK, TOK)
     for cp, ref in zip(acts, (xin, cin)):
         cp.wait()
+    for k in range(2):
+        for j, dx in enumerate((3, 1)):
+            ref = piece(x + dx, oh, odd, k)
+            copy(ref, ref, xo_s.at[k, j], xo_r.at[k, j], right).wait_recv()
+            if j == k:
+                send_piece(ref, xo_s.at[2, k], xo_r.at[2, k], (right, left)[k])
+            z_send(dx, k)
     norm(theirs)
-    x_forward(1 - yh, 1)
     x_finish(yh, 0)
-    x_finish(1 - yh, 1)
+    for k in range(2):
+        ref = piece(x + 2, oh, odd, k)
+        copy(ref, ref, xo_s.at[2, k], xo_r.at[2, k], right).wait_recv()
+        z_send(2, k)
+    for dx in (0, 3, 1, 2):
+        for k in range(2):
+            ref = piece(x + dx, oh, 1 - odd, k)
+            copy(ref, ref, za_s.at[dx, k], za_r.at[dx, k], right).wait_recv()
     for cp in x_copies:
         cp.wait_send()
 
@@ -158,7 +206,7 @@
         hb, cb = hc[0, toks, :], hc[1, toks, :]
 
         def rows(kind):
-            return wt[pl.ds(8 * kind + 4 * u, 4)].reshape(256, D)
+            return w2[blocks(8 * kind + 4 * u, 4), :]
 
         pa = lax.dot_general(rows(0), hb, NT, preferred_element_type=F32)
         pb = lax.dot_general(rows(1), hb, NT, preferred_element_type=F32)
@@ -175,34 +223,27 @@
 
     lax.fori_loop(0, 8, hidden, 0)
 
-    relocs = []
-
-    def grad_rows(k, dx):
+    def grad_rows(dx, p):
         xt = (x + dx) % NX
+        cols = pl.ds(COLS[p][0], COLS[p][1])
         for i in range(3):
             n = 3 * xt + i
             val = jnp.dot(
                 pt[pl.ds(pl.multiple_of(128 * n, 128), 128), :],
-                hc[jnp.where(n < 8, 0, 1)],
+                hc[jnp.where(n < 8, 0, 1), :, cols],
                 preferred_element_type=F32,
             ).astype(BF16)
             for e in range(2):
                 m, j = divmod(2 * i + e, 3)
-                slot = jnp.where(c == 0, (0, 2, 3)[j], (3, 0, 2)[j])
-                g4[2 * xt + m, slot] = val[64 * e : 64 * (e + 1)]
-        cp = copy(
-            g4.at[pl.ds(2 * xt, 2), 3], g4.at[pl.ds(2 * xt, 2), 1], rl_s.at[k], rl_r.at[k], other
-        )
-        cp.start()
-        relocs.append(cp)
+                g4[2 * xt + m, j, :, cols] = val[64 * e : 64 * (e + 1)]
 
     def part(m, p):
-        return g4.at[m, pl.ds(0, 3), :, pl.ds(COLS[p][0], COLS[p][1])]
+        return g4.at[m, :, :, pl.ds(COLS[p][0], COLS[p][1])]
 
     def xbuf(i, p):
         return xr.at[i, :, :, pl.ds(COLS[p][0], COLS[p][1])]
 
-    x_grad = []
+    x_grad, relocs, y_grad = [], [], []
 
     def x_send(src, i, p, to):
         cp = copy(src, xbuf(i, p), xg_s.at[i, p], xg_r.at[i, p], to)
@@ -214,54 +255,47 @@
 
     pieces = range(len(COLS))
     far, near_r, near_l = (x + 2) % NX, (x + 1) % NX, (x + 3) % NX
-    grad_rows(0, 2)
-    relocs[0].wait_recv()
-    for p in pieces:
+
+    def rows_far(p):
+        grad_rows(2, p)
         x_send(part(2 * far, p), 0, p, right)
         x_send(part(2 * far + 1, p), 1, p, left)
-    grad_rows(1, 1)
-    grad_rows(2, 3)
-    relocs[1].wait_recv()
-    relocs[2].wait_recv()
-    for p in pieces:
+
+    def rows_near(p):
+        grad_rows(1, p)
         x_send(part(2 * near_r + 1, p), 2, p, right)
+        grad_rows(3, p)
         x_send(part(2 * near_l, p), 3, p, left)
-    grad_rows(3, 0)
-
-    for p in pieces:
+        grad_rows(0, p)
+
+    def x_pass(p):
         cols = pl.ds(COLS[p][0], COLS[p][1])
         for i, m, to in ((0, 2 * near_r, right), (1, 2 * near_l + 1, left)):
             x_wait(i, p)
-            tot = g4[m, 0:3, :, cols].astype(F32) + xr[i, :, :, cols].astype(F32)
-            g4[m, 0:3, :, cols] = tot.astype(BF16)
+            tot = g4[m, :, :, cols].astype(F32) + xr[i, :, :, cols].astype(F32)
+            g4[m, :, :, cols] = tot.astype(BF16)
             x_send(part(m, p), 4 + i, p, to)
 
-    def dh_rows(t0):
-        def step(i, _):
-            toks = pl.ds(pl.multiple_of(t0 + i * 256, 256), 256)
-            dh[toks, :] = lax.dot_general(
-                pt[pl.ds(0, 1024), toks], wt[0:16].reshape(1024, D), TN, preferred_element_type=F32
-            )
-            return 0
-
-        lax.fori_loop(0, 2, step, 0)
-
-    dh_rows(theirs)
-    dh_copy = copy(dh.at[pl.ds(theirs, TOK)], dhr, dh_s, dh_r, other)
-    dh_copy.start()
-    dh_rows(mine)
-    relocs[3].wait_recv()
-
-    y_grad = []
-    for p in pieces:
+    def x_done(p):
         cols = pl.ds(COLS[p][0], COLS[p][1])
         for i, (one, two) in enumerate(((4, 3), (2, 5))):
-            x_wait(one, p)
-            x_wait(two, p)
-            tot = g4[2 * x + i, 0:3, :, cols].astype(F32) + xr[one, :, :, cols].astype(F32)
-            tot = tot + xr[two, :, :, cols].astype(F32)
-            s2[i, :, cols] = tot.reshape(192, COLS[p][1]).astype(BF16)
-        for d in range(1, NY):
+            x_wait(two if i == 0 else one, p)
+            x_wait(one if i == 0 else two, p)
+            tot = g4[2 * x + i, :, :, cols].astype(F32) + xr[one, :, :, cols].astype(F32)
+            tot = (tot + xr[two, :, :, cols].astype(F32)).astype(BF16)
+            for j in range(3):
+                slot = jnp.where(c == 0, (0, 2, 3)[j], (3, 0, 2)[j])
+                s2[i, pl.ds(pl.multiple_of(64 * slot, 64), 64), cols] = tot[j]
+        cp = copy(
+            s2.at[:, pl.ds(192, 64), cols], s2.at[:, pl.ds(64, 64), cols], rl_s.at[p], rl_r.at[p], other
+        )
+        cp.start()
+        relocs.append(cp)
+
+    def y_start(p):
+        cols = pl.ds(COLS[p][0], COLS[p][1])
+        relocs[p].wait_recv()
+        for d in (4, 3, 5, 2, 6, 1, 7):
             yt = (y + d) % NY
             cp = copy(
                 s2.at[yt // 4, pl.ds(pl.multiple_of(48 * (yt % 4), 16), 48), cols],
@@ -273,6 +307,37 @@
             cp.start()
             y_grad.append(cp)
 
+    def dh_rows(t0):
+        def step(i, _):
+            toks = pl.ds(pl.multiple_of(t0 + i * 256, 256), 256)
+            dh[toks, :] = lax.dot_general(
+                pt[pl.ds(0, 1024), toks], w2[0:1024, :], TN, preferred_element_type=F32
+            )
+            return 0
+
+        lax.fori_loop(0, 2, step, 0)
+
+    last = len(COLS) - 1
+    rows_far(0)
+    rows_near(0)
+    for p in range(1, last + 1):
+        rows_far(p)
+        x_pass(p - 1)
+        rows_near(p)
+        if p >= 2:
+            x_done(p - 2)
+            y_start(p - 2)
+    if last >= 1:
+        x_done(last - 1)
+        y_start(last - 1)
+    x_pass(last)
+    dh_rows(theirs)
+    dh_copy = copy(dh.at[pl.ds(theirs, TOK)], dhr, dh_s, dh_r, other)
+    dh_copy.start()
+    x_done(last)
+    y_start(last)
+    dh_rows(mine)
+
     dh_copy.wait()
 
     def finish_input(i, _):
@@ -331,27 +396,25 @@
         tot = tot + zr[zf].astype(F32)
 
     grad = tot[0:30] * (1.0 / 512.0)
-    n1 = 0.9 * mo1[...] + 0.1 * grad
-    n2 = 0.95 * mo2[...] + 0.05 * grad * grad
-    nm = mas[...] - 0.01 * (n1 / (jnp.sqrt(n2) + 1e-8) + 0.1 * mas[...])
+    n1 = 0.9 * state[1] + 0.1 * grad
+    n2 = 0.95 * state[2] + 0.05 * grad * grad
+    nm = state[0] - 0.01 * (n1 / (jnp.sqrt(n2) + 1e-8) + 0.1 * state[0])
     nb[pl.ds(0, 30), :] = nm
     nb[pl.ds(30, 2), :] = jnp.zeros((2, 128), F32)
-    nw_o[b] = nb[...].astype(BF16)
+    nwr[b] = nb[...].astype(BF16)
     new = []
-    for dz in range(NZ):
-        for dq in range(NQ):
-            if dz or dq:
-                zt = (z + dz) % NZ
-                cp = copy(
-                    nw_o.at[b], nw_o.at[b], nw_s.at[dz, dq], nw_r.at[dz, dq],
-                    dev(z_to=zt, y_to=yh * 4 + (q + dq) % NQ),
-                )
-                cp.start()
-                new.append(cp)
-    grad_o[...] = grad
-    n1_o[...] = n1
-    n2_o[...] = n2
-    nm_o[...] = nm
+    near_first = [(dz, dq) for dz in range(NZ) for dq in range(NQ) if dz or dq]
+    near_first.sort(key=lambda v: (min(v[0], NZ - v[0]) + v[1], v))
+    for dz, dq in near_first[::-1]:
+        cp = copy(
+            nwr.at[b], nwr.at[b], nw_s.at[dz, dq], nw_r.at[dz, dq],
+            dev(z_to=(z + dz) % NZ, y_to=yh * 4 + (q + dq) % NQ),
+        )
+        cp.start()
+        new.append(cp)
+    for ref, val in ((grad_o, grad), (n1_o, n1), (n2_o, n2), (nm_o, nm)):
+        for r in range(30):
+            ref[:, pl.ds(128 * r, 128)] = val[r : r + 1]
 
     for cp in relocs + x_grad + y_grad:
         cp.wait_send()
@@ -363,11 +426,16 @@
             def _():
                 copy(zb.at[e * 4 + qt], zr.at[z], zg_s.at[e * 4 + qt], zg_r.at[z], right).wait_send()
 
-    for dz in range(NZ):
-        for dq in range(NQ):
-            if dz or dq:
-                bf = ((z - dz + NZ) % NZ) * 4 + (q - dq + NQ) % NQ
-                copy(nw_o.at[bf], nw_o.at[bf], nw_s.at[dz, dq], nw_r.at[dz, dq], right).wait_recv()
+    def lay_flat(i):
+        rows = nwr[i].astype(F32)
+        for r in range(30):
+            nw_o[:, pl.ds(pl.multiple_of(3840 * i + 128 * r, 128), 128)] = rows[r : r + 1].astype(BF16)
+
+    lay_flat(b)
+    for dz, dq in near_first:
+        bf = ((z - dz + NZ) % NZ) * 4 + (q - dq + NQ) % NQ
+        copy(nwr.at[bf], nwr.at[bf], nw_s.at[dz, dq], nw_r.at[dz, dq], right).wait_recv()
+        lay_flat(bf)
     for cp in new:
         cp.wait_send()
 
@@ -376,28 +444,31 @@
     vm = pl.BlockSpec(memory_space=pltpu.VMEM)
     dma = pltpu.SemaphoreType.DMA
     np_ = len(COLS)
-    state = [v.reshape(30, 128) for v in (master, moment_one, moment_two)]
     shape = jax.ShapeDtypeStruct
     gin, grad, nw, nm, n1, n2 = pl.pallas_call(
         mesh_kernel,
         out_shape=[
             shape((TOK, D), BF16),
-            shape((30, 128), F32),
-            shape((32, 32, 128), BF16),
-            shape((30, 128), F32),
-            shape((30, 128), F32),
-            shape((30, 128), F32),
+            shape((1, 3840), F32),
+            shape((1, 32 * 3840), BF16),
+            shape((1, 3840), F32),
+            shape((1, 3840), F32),
+            shape((1, 3840), F32),
         ],
         in_specs=[vm] * 7,
         out_specs=[vm] * 6,
         scratch_shapes=[
+            pltpu.VMEM((3 * BLK, D), F32),
+            pltpu.VMEM((BLK, D), BF16),
+            pltpu.VMEM((3, 30, 128), F32),
+            pltpu.VMEM((32, 32, 128), BF16),
             pltpu.VMEM((2 * TOK, D), BF16),
             pltpu.VMEM((2 * TOK, D), BF16),
             pltpu.VMEM((2, 2 * TOK, D), BF16),
-            pltpu.VMEM((24, BLK, D), BF16),
+            pltpu.VMEM((24 * BLK, D), BF16),
             pltpu.VMEM((1536, 2 * TOK), BF16),
-            pltpu.VMEM((8, 4, BLK, D), BF16),
-            pltpu.VMEM((2, 192, D), BF16),
+            pltpu.VMEM((8, 3, BLK, D), BF16),
+            pltpu.VMEM((2, 256, D), BF16),
             pltpu.VMEM((6, 3, BLK, D), BF16),
             pltpu.VMEM((NY, 48, D), BF16),
             pltpu.VMEM((48, D), F32),
@@ -410,9 +481,11 @@
             pltpu.VMEM((2 * TOK, 128), F32),
             dma((2,)), dma((2,)),
             dma, dma,
-            dma((2,)), dma,
-            dma((2, 4)), dma((2, 4)),
-            dma((4,)), dma((4,)),
+            dma((2, 2)), dma((2,)),
+            dma((1, 4)), dma((1, 4)),
+            dma((3, 2)), dma((3, 2)),
+            dma((NX, 2)), dma((NX, 2)),
+            dma((np_,)), dma((np_,)),
             dma((6, np_)), dma((6, np_)),
             dma((NY, np_)), dma((NY, np_)),
             dma((8,)), dma((NZ,)),
@@ -423,16 +496,24 @@
             collective_id=0, has_side_effects=True, vmem_limit_bytes=56 * 1024 * 1024
         ),
         name="ffn_backward_adam",
-    )(activations, upstream, norm_gain, weight_shards.reshape(3, BLK, D), *state)
-    flat = lambda v: v.reshape(1, 3840)
-    return (
-        gin,
-        flat(grad),
-        nw[:, :30].reshape(1, 32 * 3840),
-        flat(nm),
-        flat(n1),
-        flat(n2),
-    )
+    )(activations, upstream, norm_gain, weight_shards, master, moment_one, moment_two)
+    return emit(gin, grad, nw, nm, n1, n2)
+
+
+def emit_kernel(*refs):
+    for src, dst in zip(refs[:6], refs[6:]):
+        dst[...] = src[...]
+
+
+def emit(*arrays):
+    vm = pl.BlockSpec(memory_space=pltpu.VMEM)
+    return pl.pallas_call(
+        emit_kernel,
+        out_shape=[jax.ShapeDtypeStruct(v.shape, v.dtype) for v in arrays],
+        in_specs=[vm] * 6,
+        out_specs=[vm] * 6,
+        name="emit",
+    )(*arrays)
 
 
 def solution(mesh):

time: 106 us -> 88.9 us (0.84)
  local copies, waits for them, and re-layouts: 6.53 us -> 0 us
  Pallas kernels: 93.4 us -> 88.1 us
  other arithmetic: 4.3 us -> 0 us
    reshape x4 -> x0, local copies, waits for them, and re-layouts: 5.53 us -> none  [the longest x2 2.81 us: shards(): flat = lambda v: v.reshape(1, 3840)]
    pallas_call x1 -> x2, Pallas kernels: 93.4 us -> 88.1 us  [the longest x1 85.8 us: shards(): pl.pallas_call(mesh_kernel, out_shape=[shape((TOK, D), BF16), shape((1, 3...]
    unnamed x4 -> x0, other arithmetic: 4.3 us -> none
where the time goes in v2:
time: 88.9 us; the launch traced here: 88.8 us
  Pallas kernels  88.1 us (99%)
    pallas_call x1, Pallas kernels, shards(): pl.pallas_call(mesh_kernel, out_shape=[shape((TOK, D), BF16), shape((1, 3...  85.8 us
    pallas_call x1, Pallas kernels, emit(): pl.pallas_call(emit_kernel, out_shape=[jax.ShapeDtypeStruct(v.shape, v.dt...  2.32 us

profile of v2, /device:TPU:1, one launch (start us, length us, event | category | flops | bytes accessed | tf_op | source)
XLA Modules:
  0.0 88.8 jit_solution(16812010992516297214)
XLA Ops:
  0.6 85.8 %ffn_backward_adam.1 = (bf16[512,640]{1,0:T(8,128)(2,1)}, f32[1,3840]{1,0:T(1,128)}, bf16[1,122880]{1,0:T(2,128)(2,1)}, f32[1,3840]{1,0:T(1,128)}, f32[1,3840]{1,0:T(1,128)}, /*index=5*/f32[1,3840]{1,0:T(1,128)}) custom-call(bf16[512,640]{1,0:T(8,128)(2,1)} %act.1, bf16[512,640]{1,0:T(8,128)(2,1)} %up.1, f32[1,640]{1,0:T(1,128)} %gain.1, ...), custom_call_target="tpu_custom_call" | custom-call | tf_op jit(solution)/shard_map/ffn_backward_adam/pallas_call | solution.py:448
  86.4 2.3 %emit.1 = (bf16[512,640]{1,0:T(8,128)(2,1)}, f32[1,3840]{1,0:T(1,128)}, bf16[1,122880]{1,0:T(2,128)(2,1)}, f32[1,3840]{1,0:T(1,128)}, f32[1,3840]{1,0:T(1,128)}, /*index=5*/f32[1,3840]{1,0:T(1,128)}) custom-call(bf16[512,640]{1,0:T(8,128)(2,1)} %get-tuple-element.12.refs_0_, f32[1,3840]{1,0:T(1,128)} %get-tuple-element.13.refs_1_, ...), custom_call_target="tpu_custom_call" | custom-call | tf_op jit(solution)/shard_map/emit/pallas_call | solution.py:510

commit v3 on v2

--- a/solution.py
+++ b/solution.py
@@ -15,7 +15,7 @@
 TOK = 512
 NX, NY, NZ, NQ = 4, 8, 8, 4
 BLK = 64
-COLS = ((0, 256), (256, 256), (512, 128))
+COLS = ((0, 128), (128, 256), (384, 128), (512, 128))
 
 NT = (((1,), (1,)), ((), ()))
 TN = (((0,), (0,)), ((), ()))
@@ -27,7 +27,7 @@
     act, up, gain, wflat, mas, mo1, mo2,
     gin_o, grad_o, nw_o, nm_o, n1_o, n2_o,
     wf, wsh, state, nwr, xin, cin, hc, w2, pt, g4, s2, xr, yr, tsum, zs, zb, zr, nb, dh, dhr, invr,
-    act_s, act_r, a1_s, a1_r, ya_s, ya_r, xa_s, xa_r, xo_s, xo_r, za_s, za_r, rl_s, rl_r, xg_s, xg_r, yg_s, yg_r,
+    ld_s, act_s, act_r, a1_s, a1_r, ya_s, ya_r, xa_s, xa_r, xo_s, xo_r, za_s, za_r, rl_s, rl_r, xg_s, xg_r, yg_s, yg_r,
     zg_s, zg_r, dh_s, dh_r, nw_s, nw_r,
 ):
     a = lax.axis_index("dpa")
@@ -62,8 +62,12 @@
     def blocks(t, n=1):
         return pl.ds(pl.multiple_of(BLK * t, BLK), BLK * n)
 
-    xin[pl.ds(mine, TOK), :] = act[...]
-    cin[pl.ds(mine, TOK), :] = up[...]
+    loads = [
+        pltpu.make_async_copy(src, dst.at[pl.ds(mine, TOK)], ld_s.at[i])
+        for i, (src, dst) in enumerate(((act, xin), (up, cin)))
+    ]
+    for cp in loads:
+        cp.start()
     for r in range(3 * BLK):
         wf[pl.ds(r, 1), :] = wflat[:, pl.ds(D * r, D)].astype(F32)
     w2[blocks(own_t + c)] = wf[0:64].astype(BF16)
@@ -81,7 +85,8 @@
         copy(ref.at[pl.ds(mine, TOK)], ref.at[pl.ds(mine, TOK)], act_s.at[i], act_r.at[i], other)
         for i, ref in enumerate((xin, cin))
     ]
-    for cp in acts:
+    for cp, load in zip(acts, loads):
+        load.wait()
         cp.start()
     a1.wait()
 
@@ -455,7 +460,7 @@
             shape((1, 3840), F32),
             shape((1, 3840), F32),
         ],
-        in_specs=[vm] * 7,
+        in_specs=[pl.BlockSpec(memory_space=pl.ANY)] * 2 + [vm] * 5,
         out_specs=[vm] * 6,
         scratch_shapes=[
             pltpu.VMEM((3 * BLK, D), F32),
@@ -479,6 +484,7 @@
             pltpu.VMEM((2 * TOK, D), F32),
             pltpu.VMEM((TOK, D), F32),
             pltpu.VMEM((2 * TOK, 128), F32),
+            dma((2,)),
             dma((2,)), dma((2,)),
             dma, dma,
             dma((2, 2)), dma((2,)),

time: 88.9 us -> 86.5 us (0.973)
  Pallas kernels: 88.1 us -> 85.2 us
    pallas_call x1, Pallas kernels: 85.8 us -> 82.9 us  [shards(): pl.pallas_call(mesh_kernel, out_shape=[shape((TOK, D), BF16), shape((1, 3...]
where the time goes in v3:
time: 86.5 us; the launch traced here: 85.8 us
  Pallas kernels  85.2 us (98%)
    pallas_call x1, Pallas kernels, shards(): pl.pallas_call(mesh_kernel, out_shape=[shape((TOK, D), BF16), shape((1, 3...  82.9 us
    pallas_call x1, Pallas kernels, emit(): pl.pallas_call(emit_kernel, out_shape=[jax.ShapeDtypeStruct(v.shape, v.dt...  2.32 us

profile of v3, /device:TPU:1, one launch (start us, length us, event | category | flops | bytes accessed | tf_op | source)
XLA Modules:
  0.0 85.8 jit_solution(8456547180518682151)
XLA Ops:
  0.6 82.9 %ffn_backward_adam.1 = (bf16[512,640]{1,0:T(8,128)(2,1)}, f32[1,3840]{1,0:T(1,128)}, bf16[1,122880]{1,0:T(2,128)(2,1)}, f32[1,3840]{1,0:T(1,128)}, f32[1,3840]{1,0:T(1,128)}, /*index=5*/f32[1,3840]{1,0:T(1,128)}) custom-call(bf16[512,640]{1,0:T(8,128)(2,1)} %act.1, bf16[512,640]{1,0:T(8,128)(2,1)} %up.1, f32[1,640]{1,0:T(1,128)} %gain.1, ...), custom_call_target="tpu_custom_call" | custom-call | tf_op jit(solution)/shard_map/ffn_backward_adam/pallas_call | solution.py:453
  83.5 2.3 %emit.1 = (bf16[512,640]{1,0:T(8,128)(2,1)}, f32[1,3840]{1,0:T(1,128)}, bf16[1,122880]{1,0:T(2,128)(2,1)}, f32[1,3840]{1,0:T(1,128)}, f32[1,3840]{1,0:T(1,128)}, /*index=5*/f32[1,3840]{1,0:T(1,128)}) custom-call(bf16[512,640]{1,0:T(8,128)(2,1)} %get-tuple-element.12.refs_0_, f32[1,3840]{1,0:T(1,128)} %get-tuple-element.13.refs_1_, ...), custom_call_target="tpu_custom_call" | custom-call | tf_op jit(solution)/shard_map/emit/pallas_call | solution.py:516

commit v4 on v3

--- a/solution.py
+++ b/solution.py
@@ -322,25 +322,29 @@
 
         lax.fori_loop(0, 2, step, 0)
 
-    last = len(COLS) - 1
     rows_far(0)
     rows_near(0)
-    for p in range(1, last + 1):
-        rows_far(p)
-        x_pass(p - 1)
-        rows_near(p)
-        if p >= 2:
-            x_done(p - 2)
-            y_start(p - 2)
-    if last >= 1:
-        x_done(last - 1)
-        y_start(last - 1)
-    x_pass(last)
+    rows_far(1)
+    x_pass(0)
+    rows_near(1)
+    rows_far(2)
+    x_pass(1)
+    rows_near(2)
+    x_done(0)
+    y_start(0)
+    rows_far(3)
+    x_pass(2)
+    rows_near(3)
+    x_done(1)
+    y_start(1)
+    x_pass(3)
+    x_done(2)
+    y_start(2)
     dh_rows(theirs)
     dh_copy = copy(dh.at[pl.ds(theirs, TOK)], dhr, dh_s, dh_r, other)
     dh_copy.start()
-    x_done(last)
-    y_start(last)
+    x_done(3)
+    y_start(3)
     dh_rows(mine)
 
     dh_copy.wait()

time: 86.5 us -> 86.1 us (level)
  no operation moved by 1% of the time
where the time goes in v4:
time: 86.1 us; the launch traced here: 85.1 us
  Pallas kernels  84.5 us (98%)
    pallas_call x1, Pallas kernels, shards(): pl.pallas_call(mesh_kernel, out_shape=[shape((TOK, D), BF16), shape((1, 3...  82.2 us
    pallas_call x1, Pallas kernels, emit(): pl.pallas_call(emit_kernel, out_shape=[jax.ShapeDtypeStruct(v.shape, v.dt...  2.32 us

profile of v4, /device:TPU:1, one launch (start us, length us, event | category | flops | bytes accessed | tf_op | source)
XLA Modules:
  0.0 85.1 jit_solution(11366044575115507061)
XLA Ops:
  0.6 82.2 %ffn_backward_adam.1 = (bf16[512,640]{1,0:T(8,128)(2,1)}, f32[1,3840]{1,0:T(1,128)}, bf16[1,122880]{1,0:T(2,128)(2,1)}, f32[1,3840]{1,0:T(1,128)}, f32[1,3840]{1,0:T(1,128)}, /*index=5*/f32[1,3840]{1,0:T(1,128)}) custom-call(bf16[512,640]{1,0:T(8,128)(2,1)} %act.1, bf16[512,640]{1,0:T(8,128)(2,1)} %up.1, f32[1,640]{1,0:T(1,128)} %gain.1, ...), custom_call_target="tpu_custom_call" | custom-call | tf_op jit(solution)/shard_map/ffn_backward_adam/pallas_call | solution.py:457
  82.8 2.3 %emit.1 = (bf16[512,640]{1,0:T(8,128)(2,1)}, f32[1,3840]{1,0:T(1,128)}, bf16[1,122880]{1,0:T(2,128)(2,1)}, f32[1,3840]{1,0:T(1,128)}, f32[1,3840]{1,0:T(1,128)}, /*index=5*/f32[1,3840]{1,0:T(1,128)}) custom-call(bf16[512,640]{1,0:T(8,128)(2,1)} %get-tuple-element.12.refs_0_, f32[1,3840]{1,0:T(1,128)} %get-tuple-element.13.refs_1_, ...), custom_call_target="tpu_custom_call" | custom-call | tf_op jit(solution)/shard_map/emit/pallas_call | solution.py:520
